TPU v7x, 32 devices: a whole 2x2x4 slice. The times are simulated.
32 devices in a mesh: groups: 2 (over y), gx: 8 (over z, x), gy: 2 (over core).
Axes of the slice: x: 2, y: 2, z: 4, core: 2. Of those that a mesh axis runs over, the one named last changes fastest.
Arguments:
- tokens: bfloat16 [32, 16384], P(('groups', 'gx'), 'gy'), parts along dimension 0, may hold values from -6 to 6
- query_weight: bfloat16 [12288, 16384], P('gx', 'gy'), may hold values from -0.046875 to 0.046875
- key_weight: bfloat16 [768, 16384], P('gx', 'gy'), may hold values from -0.046875 to 0.046875
- value_weight: bfloat16 [768, 16384], P('gx', 'gy'), may hold values from -0.046875 to 0.046875
- output_weight: bfloat16 [16384, 12288], P('gx', 'gy'), may hold values from -0.0546875 to 0.0546875
- key_cache: bfloat16 [32, 6, 256, 128], P(('groups', 'gx'), 'gy'), parts along dimension 0, may hold values from -68 to 68
- value_cache: bfloat16 [32, 6, 256, 128], P(('groups', 'gx'), 'gy'), parts along dimension 0, may hold values from -6 to 6
- lengths: int32 [32], P(('groups', 'gx')), parts along dimension 0, may hold values from 1 to 256, as said below
Outputs:
- block_out: bfloat16 [32, 16384], P(('groups', 'gy'), 'gx'), parts along dimension 0
There are 2 independent parts, one for each index of `groups`. A program takes and returns all parts, laid end to end along the dimension named above; an argument that names none is the same for every part. Nothing has to cross between parts.
Inputs may be any that keep to these rules, and one draw needn't show every extreme that they name: `lengths`: every row has at least one cached token and some row of every draw has exactly 256.
All inputs are finite; a program needn't handle non-finite values.
Results may differ from a plain program's by a relative error of at most 0.0082.
Values may be sent and summed in bfloat16 or wider, within the bound.
A program may use at most 128 MiB of HBM per device.

v0:
```python
import math

import jax
import jax.numpy as jnp
from jax import lax
from jax.sharding import PartitionSpec as P

HD = 128
HQ = 96
KVH = 6


def rotate(values, positions):
    half_width = values.shape[-1] // 2
    freqs = jnp.exp(
        -(jnp.arange(half_width, dtype=jnp.float32) * (2.0 / values.shape[-1])) * math.log(500000.0)
    )
    angles = positions[:, None] * freqs[None, :]
    cosine = jnp.cos(angles)[:, None, :]
    sine = jnp.sin(angles)[:, None, :]
    first = values[..., :half_width]
    second = values[..., half_width:]
    return jnp.concatenate(
        [first * cosine - second * sine, second * cosine + first * sine], axis=-1
    )


def product(row_piece, matrix):
    return lax.dot_general(
        row_piece, matrix, (((1,), (1,)), ((), ())), preferred_element_type=jnp.float32
    )


def local(
    tokens, query_weight, key_weight, value_weight, output_weight, key_cache, value_cache, lengths
):
    rows_here = tokens.shape[0]
    width_gx = lax.axis_size("gx")
    width_query = query_weight.shape[0]
    width_key = key_weight.shape[0]
    width_all = width_query + 2 * width_key
    local_heads = key_cache.shape[1]
    group_size = HQ // KVH
    row_piece = lax.all_gather(tokens, "gx", axis=0, tiled=True)
    partial_value = jnp.concatenate(
        [
            product(row_piece, query_weight),
            product(row_piece, key_weight),
            product(row_piece, value_weight),
        ],
        axis=1,
    )
    summed = lax.psum(partial_value, "gy").astype(jnp.bfloat16)
    owned = lax.all_to_all(summed, "gx", split_axis=0, concat_axis=1, tiled=True)
    blocks = owned.reshape(rows_here, width_gx, width_all)
    query_all = blocks[:, :, :width_query].reshape(rows_here, HQ, HD)
    key_all = blocks[:, :, width_query : width_query + width_key].reshape(rows_here, KVH, HD)
    value_all = blocks[:, :, width_query + width_key :].reshape(rows_here, KVH, HD)
    shard = lax.axis_index("gy")
    query_part = lax.dynamic_slice_in_dim(
        query_all, shard * local_heads * group_size, local_heads * group_size, 1
    )
    key_part = lax.dynamic_slice_in_dim(key_all, shard * local_heads, local_heads, 1)
    value_part = lax.dynamic_slice_in_dim(value_all, shard * local_heads, local_heads, 1)
    positions = lengths.astype(jnp.float32)
    query_rot = rotate(query_part.astype(jnp.float32), positions).astype(jnp.bfloat16)
    query_rot = query_rot.reshape(rows_here, local_heads, group_size, HD)
    key_rot = rotate(key_part.astype(jnp.float32), positions).astype(jnp.bfloat16)
    scale = HD ** (-0.5)
    own_score = (
        jnp.einsum("rgqd,rgd->rgq", query_rot, key_rot, preferred_element_type=jnp.float32) * scale
    )
    cache_len = key_cache.shape[2]
    scores = (
        jnp.einsum("rgqd,rgpd->rgqp", query_rot, key_cache, preferred_element_type=jnp.float32)
        * scale
    )
    valid_keys = jnp.arange(cache_len)[None, None, None, :] < lengths[:, None, None, None]
    scores = jnp.where(valid_keys, scores, -jnp.inf)
    peak = jnp.maximum(jnp.max(scores, axis=-1), own_score)
    exps = jnp.exp(scores - peak[..., None])
    own_exp = jnp.exp(own_score - peak)
    total = jnp.sum(exps, axis=-1) + own_exp
    weights = (exps / total[..., None]).astype(jnp.bfloat16)
    mixed = jnp.einsum("rgqp,rgpd->rgqd", weights, value_cache, preferred_element_type=jnp.float32)
    own_weight = (own_exp / total).astype(jnp.bfloat16)
    mixed = (
        mixed
        + own_weight.astype(jnp.float32)[..., None] * value_part.astype(jnp.float32)[:, :, None, :]
    )
    attended = mixed.astype(jnp.bfloat16).reshape(rows_here, local_heads * group_size * HD)
    terms = product(lax.all_gather(attended, "gx", axis=0, tiled=True), output_weight)
    return lax.psum_scatter(terms, "gy", scatter_dimension=0, tiled=True).astype(jnp.bfloat16)


def solution(mesh):
    in_specs = (
        P(("groups", "gx"), "gy"),
        P("gx", "gy"),
        P("gx", "gy"),
        P("gx", "gy"),
        P("gx", "gy"),
        P(("groups", "gx"), "gy", None, None),
        P(("groups", "gx"), "gy", None, None),
        P(("groups", "gx")),
    )
    out_specs = P(("groups", "gy"), "gx")
    return jax.shard_map(local, mesh=mesh, in_specs=in_specs, out_specs=out_specs, check_vma=False)
```

profile of v0, /device:TPU:0, one launch (start us, length us, event | category | flops | bytes accessed | tf_op | source)
XLA Modules:
  0.0 132.1 jit_solution(4115751746442819824)
XLA Ops:
  6.5 0.0 copy-start
  6.5 0.0 copy-start.1
  6.5 34.9 %all-gather = bf16[8,2,8192]{2,1,0:T(2,128)(2,1)} all-gather(bf16[1,2,8192]{2,1,0:T(2,128)(2,1)} %bitcast.40), channel_id=1, replica_groups=mesh['groups'=2,'gx'=8,'gy'=2] {'gx'}, dimensions={0}, use_global_device_ids=true | all-gather | bytes 294912 | tf_op jit(solution)/shard_map/all_gather | solution.py:44
  41.4 0.0 copy-start.2
  41.4 1.1 reshape.104
  42.5 11.5 %fusion.14 = f32[16,1536]{1,0:T(8,128)S(1)} fusion(bf16[16,8192]{1,0:T(8,128)(2,1)S(1)} %reshape.104, bf16[1536,8192]{1,0:T(8,128)(2,1)} %param.9), kind=kOutput, calls=%fused_computation.34 | convolution fusion | flops 402653184 | bytes 25526272 | tf_op jit(solution)/shard_map/dot_general | solution.py:29
  54.0 0.0 copy-done
  54.0 0.5 fusion.15
  54.5 0.0 copy-done.1
  54.5 0.5 fusion.16
  55.0 0.1 concatenate.16
  55.1 3.8 %psum.7 = bf16[16,1728]{1,0:T(8,128)(2,1)S(1)} all-reduce(f32[16,1728]{1,0:T(8,128)S(1)} %concatenate.16), channel_id=1, replica_groups=mesh['groups'=2,'gx'=8,'gy'=2] {'gy'}, use_global_device_ids=true, to_apply=%region_0.0 | all-reduce | flops 27648 | bytes 165888 | tf_op jit(solution)/shard_map/psum | solution.py:53
  58.9 0.6 all_to_all.12
  59.5 5.5 %all-to-all-start = ((bf16[8,2,1728]{2,1,0:T(2,128)(2,1)}), bf16[8,2,1728]{2,1,0:T(2,128)(2,1)S(1)}, u32[]{:S(2)}, u32[]{:S(2)}) async-start(bf16[8,2,1728]{2,1,0:T(2,128)(2,1)} %all_to_all.12), calls=%async_computation | async-start | bytes 114688 | tf_op jit(solution)/shard_map/all_to_all | solution.py:54
  65.0 0.0 reduce-scatter.2.cloned.1.call-start
  65.1 0.0 copy-done.2
  65.1 0.1 multiply_cosine_fusion
  65.2 0.1 iota_compare_fusion
  65.3 6.6 %all-to-all-done = bf16[8,2,1728]{2,1,0:T(2,128)(2,1)S(1)} async-done(((bf16[8,2,1728]{2,1,0:T(2,128)(2,1)}), bf16[8,2,1728]{2,1,0:T(2,128)(2,1)S(1)}, u32[]{:S(2)}, u32[]{:S(2)}) %all-to-all-start) | async-done | bytes 55328 | tf_op jit(solution)/shard_map/all_to_all | solution.py:54
  71.9 0.1 fusion.12
  72.0 0.1 reshape.99
  72.1 0.1 reshape.101
  72.2 0.1 reshape.100
  72.3 0.1 subtract_convert_fusion
  72.4 0.1 subtract_convert_fusion.1
  72.5 0.1 maximum_bitcast_fusion
  72.6 0.2 fusion.6
  72.8 1.3 %fusion.13 = (f32[2,3,16]{2,1,0:T(4,128)S(1)}, f32[2,3,16,256]{3,2,1,0:T(8,128)S(1)}) fusion(bf16[2,3,256,128]{3,2,1,0:T(8,128)(2,1)} %param.13, bf16[2,3,16,64]{3,2,1,0:T(8,128)(2,1)S(1)} %bitcast.39, bf16[2,3,16,64]{3,2,1,0:T(8,128)(2,1)S(1)} %bitcast.37, pred[2,256]{1,0:T(4,128)(4,1)S(1)} %iota_compare_fusion), kind=kOutput, calls=%fused_computation.33 | convolution fusion | flops 6414240 | bytes 516992 | tf_op jit(solution)/shard_map/rgqd,rgpd->rgqp/dot_general | solution.py:75
  74.1 0.2 fusion.2
  74.3 1.2 fusion.1
  75.6 30.6 %all-gather.1 = bf16[8,2,6144]{2,1,0:T(2,128)(2,1)S(1)} all-gather(bf16[1,2,6144]{2,1,0:T(2,128)(2,1)S(1)} %reshape.105), channel_id=1, replica_groups=mesh['groups'=2,'gx'=8,'gy'=2] {'gx'}, dimensions={0}, use_global_device_ids=true | all-gather | bytes 221184 | tf_op jit(solution)/shard_map/all_gather | solution.py:92
  106.2 0.1 reshape.106
  106.3 12.2 %fusion.17 = f32[16,2048]{1,0:T(8,128)} fusion(bf16[16,6144]{1,0:T(8,128)(2,1)S(1)} %reshape.106, bf16[2048,6144]{1,0:T(8,128)(2,1)} %param.12), kind=kOutput, calls=%fused_computation.37 | convolution fusion | flops 402653184 | bytes 25493504 | tf_op jit(solution)/shard_map/dot_general | solution.py:29
  118.4 0.0 reduce-scatter.2.cloned.1.call-update
  118.5 5.3 %reduce-scatter.2.cloned.1.call-done = f32[8,2048]{1,0:T(8,128)} async-done(((f32[16,2048]{1,0:T(8,128)}), f32[8,2048]{1,0:T(8,128)}) %reduce-scatter.2.cloned.1.call-update) | async-done | bytes 65552 | tf_op jit(solution)/shard_map/reduce_scatter | solution.py:93
  123.8 1.5 %convert_element_type.42 = bf16[8,2048]{1,0:T(8,128)(2,1)} convert(f32[8,2048]{1,0:T(8,128)} %reduce-scatter.2.cloned.1.call-done) | non-fusion elementwise | flops 16384 | bytes 98304 | tf_op jit(solution)/shard_map/convert_element_type | solution.py:93
  (11 shorter events, 0.1 us)
Async XLA Ops:
  6.5 47.4 %copy-start = (bf16[96,8192]{1,0:T(8,128)(2,1)S(1)}, bf16[96,8192]{1,0:T(8,128)(2,1)}, u32[]{:S(2)}) copy-start(bf16[96,8192]{1,0:T(8,128)(2,1)} %param.10) | copy-start | bytes 4718596
  6.5 48.0 %copy-start.1 = (bf16[96,8192]{1,0:T(8,128)(2,1)S(1)}, bf16[96,8192]{1,0:T(8,128)(2,1)}, u32[]{:S(2)}) copy-start(bf16[96,8192]{1,0:T(8,128)(2,1)} %param.11) | copy-start | bytes 4718596
  41.4 23.7 %copy-start.2 = (s32[2]{0:T(128)S(1)}, s32[2]{0:T(128)}, u32[]{:S(2)}) copy-start(s32[2]{0:T(128)} %param.15) | copy-start | bytes 28
  59.5 12.3 %all-to-all-start = ((bf16[8,2,1728]{2,1,0:T(2,128)(2,1)}), bf16[8,2,1728]{2,1,0:T(2,128)(2,1)S(1)}, u32[]{:S(2)}, u32[]{:S(2)}) async-start(bf16[8,2,1728]{2,1,0:T(2,128)(2,1)} %all_to_all.12), calls=%async_computation | async-start | bytes 114688 | tf_op jit(solution)/shard_map/all_to_all | solution.py:54
  65.0 58.7 %reduce-scatter.2.cloned.1.call-start = ((), (), s32[]{:S(2)}) async-start(), calls=%async_computation.2 | async-start | bytes 196608 | tf_op jit(solution)/shard_map/reduce_scatter | solution.py:93
Sparse Core Ops, SparseCore 0:
  118.6 5.1 reduce-scatter.1
where the time goes:
time: 132 us
  blocking collectives  69.3 us (52%)
  matrix products  27.5 us (21%)
  between operations  13.5 us (10%)
  waiting for transfers between devices  11.9 us (9%)
  starting transfers between devices  5.5 us (4%)
  local copies, waits for them, and re-layouts  2.29 us (2%)
  other arithmetic  2.12 us (2%)
    all_gather x1, blocking collectives, local(): row_piece = lax.all_gather(tokens, 'gx', axis=0, tiled=True)  34.9 us
    all_gather x1, blocking collectives, local(): lax.all_gather(attended, 'gx', axis=0, tiled=True)  30.6 us
    dot_general x4, matrix products, product(): lax.dot_general(row_piece, matrix, (((1,), (1,)), ((), ())), preferred_el...  24.7 us
    all_to_all x1, waiting for transfers between devices, local(): lax.all_to_all(summed, 'gx', split_axis=0, concat_axis=1, tiled=True)  6.59 us
    all_to_all x1, starting transfers between devices, local(): lax.all_to_all(summed, 'gx', split_axis=0, concat_axis=1, tiled=True)  5.46 us
    reduce_scatter x1, waiting for transfers between devices, local(): lax.psum_scatter(terms, 'gy', scatter_dimension=0, tiled=True)  5.28 us
    psum x1, blocking collectives, local(): summed = lax.psum(partial_value, 'gy').astype(jnp.bfloat16)  3.78 us
  transfers between devices with their start and end apart: 2, of which 2 were waited for; matrix products, arithmetic and copies ran while one was open for 0% of the time, Pallas kernels for 0%

commit v1 on v0

--- a/solution.py
+++ b/solution.py
@@ -3,11 +3,324 @@
 import jax
 import jax.numpy as jnp
 from jax import lax
+from jax.experimental import pallas as pl
+from jax.experimental.pallas import tpu as pltpu
 from jax.sharding import PartitionSpec as P
 
 HD = 128
 HQ = 96
 KVH = 6
+MESH = pl.DeviceIdType.MESH
+NT = (((1,), (1,)), ((), ()))
+
+GX = 8
+TOK_ROWS = 128
+Q_CHUNK = 256
+O_CHUNK = 256
+
+
+def gather_start(buf, size, z, x, send, recv):
+    me = 2 * z + x
+    slot = buf.at[pl.ds(pl.multiple_of(me * size, size), size)]
+    copies = []
+    for d in (2, 1, 3):
+        copies.append(
+            pltpu.make_async_remote_copy(
+                slot, slot, send.at[d - 1], recv.at[me],
+                device_id={"gx": 2 * lax.rem(z + d, 4) + x}, device_id_type=MESH,
+            )
+        )
+    copies.append(
+        pltpu.make_async_remote_copy(
+            slot, slot, send.at[3], recv.at[me],
+            device_id={"gx": 2 * z + 1 - x}, device_id_type=MESH,
+        )
+    )
+    for copy in copies:
+        copy.start()
+    return copies
+
+
+def gather_finish(buf, size, z, x, send, recv):
+    other = 2 * z + 1 - x
+
+    def piece(s):
+        return buf.at[pl.ds(pl.multiple_of(s * size, size), size)]
+
+    copies = []
+    for d in (1, 3, 2):
+        s = 2 * lax.rem(z + d, 4) + x
+        copy = pltpu.make_async_remote_copy(
+            piece(s), piece(s), send.at[3 + d], recv.at[s],
+            device_id={"gx": other}, device_id_type=MESH,
+        )
+        copy.wait_recv()
+        copy.start()
+        copies.append(copy)
+    for d in range(4):
+        s = 2 * lax.rem(z + d, 4) + 1 - x
+        pltpu.make_async_remote_copy(
+            piece(s), piece(s), send.at[3], recv.at[s],
+            device_id={"gx": other}, device_id_type=MESH,
+        ).wait_recv()
+    return copies
+
+
+def kernel(
+    len_ref, tok_ref, wq_hbm, wk_hbm, wv_hbm, wo_hbm, kc_hbm, vc_hbm, out_ref,
+    wq, wkv, wo, kc, vc, tok_f, xr, xf, xb, part, other_part, summed, got, qs, ag, agf, ab,
+    terms, other_terms,
+    wq_sem, wkv_sem, wo_sem, c_sem, x_send, x_recv, p_send, p_recv, m_send, m_recv,
+    a_send, a_recv, t_send, t_recv,
+):
+    i = lax.axis_index("gx")
+    c = lax.axis_index("gy")
+    z, x = i // 2, lax.rem(i, 2)
+    half = i // 4
+    n_q, n_o = wq.shape[0], wo.shape[0]
+    kw = wk_hbm.shape[0]
+
+    def wq_copy(t):
+        return pltpu.make_async_copy(wq_hbm.at[pl.ds(pl.multiple_of(t * Q_CHUNK, Q_CHUNK), Q_CHUNK)], wq.at[t], wq_sem.at[t])
+
+    def wo_copy(t):
+        return pltpu.make_async_copy(wo_hbm.at[pl.ds(pl.multiple_of(t * O_CHUNK, O_CHUNK), O_CHUNK)], wo.at[t], wo_sem.at[t])
+
+    wk_copy = pltpu.make_async_copy(wk_hbm, wkv.at[pl.ds(0, kw)], wkv_sem.at[0])
+    wv_copy = pltpu.make_async_copy(wv_hbm, wkv.at[pl.ds(128, kw)], wkv_sem.at[1])
+    wk_copy.start()
+    wv_copy.start()
+    for t in range(n_q):
+        wq_copy(t).start()
+    kc_copy = pltpu.make_async_copy(kc_hbm, kc, c_sem.at[0])
+    vc_copy = pltpu.make_async_copy(vc_hbm, vc, c_sem.at[1])
+    kc_copy.start()
+    vc_copy.start()
+
+    barrier = pltpu.get_barrier_semaphore()
+    for o in range(1, 2 * GX):
+        at = lax.rem(i * 2 + c + o, 2 * GX)
+        pl.semaphore_signal(
+            barrier, inc=1, device_id={"gx": at // 2, "gy": lax.rem(at, 2)}, device_id_type=MESH
+        )
+    tok = tok_ref[...].astype(jnp.float32)
+    pieces = tok.shape[1] // HD
+    for k in range(pieces):
+        tok_f[pl.ds(k, 2, stride=pieces), :] = tok[:, k * HD : (k + 1) * HD]
+    xr[pl.ds(pl.multiple_of(i * TOK_ROWS, TOK_ROWS), TOK_ROWS), :] = tok_f[...].astype(jnp.bfloat16)
+    pl.semaphore_wait(barrier, 2 * GX - 1)
+
+    sends = gather_start(xr, TOK_ROWS, z, x, x_send, x_recv)
+    wkv[kw:128, :] = jnp.zeros((128 - kw, wkv.shape[1]), jnp.bfloat16)
+    wkv[128 + kw : 256, :] = jnp.zeros((128 - kw, wkv.shape[1]), jnp.bfloat16)
+    lane = lax.broadcasted_iota(jnp.int32, (8, HD), 1)
+    row_id = lax.broadcasted_iota(jnp.int32, (8, HD), 0)
+    index = lax.rem(lane, HD // 2).astype(jnp.float32)
+    freqs = jnp.exp(-(index * (2.0 / HD)) * math.log(500000.0))
+    lengths = jnp.where(row_id == 0, len_ref[0], len_ref[1])
+    angles = lengths.astype(jnp.float32) * freqs
+    cosine = jnp.cos(angles)
+    sine = jnp.sin(angles)
+    sine = jnp.where(lane < HD // 2, -sine, sine)
+    sends += gather_finish(xr, TOK_ROWS, z, x, x_send, x_recv)
+
+    xf[...] = xr[...].astype(jnp.float32)
+    for k in range(pieces):
+        xb[:, k * HD : (k + 1) * HD] = xf[pl.ds(k, 16, stride=pieces), :].astype(jnp.bfloat16)
+
+    def put(h, value):
+        part[pl.ds(h, 16, stride=16), :] = value
+
+    wk_copy.wait()
+    wv_copy.wait()
+    kv = lax.dot_general(xb[...], wkv[...], NT, preferred_element_type=jnp.float32)
+    put(12, kv[:, :128])
+    put(13, kv[:, 128:])
+    put(14, jnp.zeros((16, 128), jnp.float32))
+    put(15, jnp.zeros((16, 128), jnp.float32))
+
+    heads = Q_CHUNK // HD
+
+    @pl.loop(0, n_q)
+    def _(t):
+        wq_copy(t).wait()
+        wo_copy(t).start()
+        value = lax.dot_general(xb[...], wq[t], NT, preferred_element_type=jnp.float32)
+        for e in range(heads):
+            put(t * heads + e, value[:, e * HD : (e + 1) * HD])
+
+    for t in range(n_q, n_o):
+        wo_copy(t).start()
+
+    away = pltpu.make_async_remote_copy(
+        part.at[pl.ds(pl.multiple_of((1 - c) * 128, 128), 128)], other_part, p_send.at[0], p_recv.at[0],
+        device_id={"gy": 1 - c}, device_id_type=MESH,
+    )
+    away.start()
+    away.wait_recv()
+    summed[...] = (part[pl.ds(pl.multiple_of(c * 128, 128), 128), :] + other_part[...]).astype(jnp.bfloat16)
+
+    mine = lax.rem(i, 4)
+
+    def message(o):
+        return pltpu.make_async_remote_copy(
+            summed.at[pl.ds(o * 32, 32)], got.at[pl.ds(pl.multiple_of(mine * 32, 32), 32)],
+            m_send.at[o], m_recv.at[mine],
+            device_id={"gx": 4 * c + o, "gy": half}, device_id_type=MESH,
+        )
+
+    def message_here(o):
+        return pltpu.make_async_copy(
+            summed.at[pl.ds(o * 32, 32)], got.at[pl.ds(o * 32, 32)], m_recv.at[o]
+        )
+
+    for o in range(4):
+        itself = jnp.logical_and(c == half, mine == o)
+
+        @pl.when(itself)
+        def _():
+            message_here(o).start()
+
+        @pl.when(jnp.logical_not(itself))
+        def _():
+            message(o).start()
+
+    kc_copy.wait()
+    vc_copy.wait()
+    for s in range(4):
+        message_here(s).wait()
+    scale = HD ** (-0.5)
+    for r in range(2):
+        keys, values = [], []
+        for s in range(4):
+            block = got[s * 32 + r * 16 : s * 32 + r * 16 + 16, :].astype(jnp.float32)
+            qs[r * 48 + 12 * s : r * 48 + 12 * s + 12, :] = block[0:12, :]
+            keys.append(block[12:13, :kw])
+            values.append(block[13:14, :kw])
+        keys = jnp.concatenate(keys, axis=1)
+        values = jnp.concatenate(values, axis=1)
+        cos_r = cosine[r : r + 1, :]
+        sin_r = sine[r : r + 1, :]
+        for g in range(3):
+            k_new = keys[:, g * HD : (g + 1) * HD]
+            v_new = values[:, g * HD : (g + 1) * HD]
+            k_rot = (k_new * cos_r + pltpu.roll(k_new, HD // 2, 1) * sin_r).astype(jnp.bfloat16)
+            q = qs[r * 48 + 16 * g : r * 48 + 16 * g + 16, :]
+            q_rot = (q * cos_r + pltpu.roll(q, HD // 2, 1) * sin_r).astype(jnp.bfloat16)
+            own = jnp.sum(
+                q_rot.astype(jnp.float32) * k_rot.astype(jnp.float32), axis=1, keepdims=True
+            ) * scale
+            scores = lax.dot_general(
+                q_rot, kc[r, g], NT, preferred_element_type=jnp.float32
+            ) * scale
+            position = lax.broadcasted_iota(jnp.int32, scores.shape, 1)
+            scores = jnp.where(position < len_ref[r], scores, -jnp.inf)
+            peak = jnp.maximum(jnp.max(scores, axis=1, keepdims=True), own)
+            exps = jnp.exp(scores - peak)
+            own_exp = jnp.exp(own - peak)
+            total = jnp.sum(exps, axis=1, keepdims=True) + own_exp
+            weights = (exps / total).astype(jnp.bfloat16)
+            own_weight = (own_exp / total).astype(jnp.bfloat16).astype(jnp.float32)
+            mixed = jnp.dot(weights, vc[r, g], preferred_element_type=jnp.float32)
+            mixed = mixed + own_weight * v_new
+            ag[pl.ds(pl.multiple_of(i * 96 + r * 48 + 16 * g, 16), 16), :] = mixed.astype(jnp.bfloat16)
+
+    sends += gather_start(ag, 96, z, x, a_send, a_recv)
+    sends += gather_finish(ag, 96, z, x, a_send, a_recv)
+    agf[...] = ag[...].astype(jnp.float32)
+    for h in range(48):
+        ab[:, h * HD : (h + 1) * HD] = agf[pl.ds(h, 16, stride=48), :].astype(jnp.bfloat16)
+
+    theirs = pl.multiple_of((1 - c) * 8, 8)
+    ours = pl.multiple_of(c * 8, 8)
+
+    def term_copy(t):
+        return pltpu.make_async_remote_copy(
+            terms.at[t, pl.ds(theirs, 8)], other_terms.at[t], t_send.at[t], t_recv.at[t],
+            device_id={"gy": 1 - c}, device_id_type=MESH,
+        )
+
+    @pl.loop(0, n_o)
+    def _(t):
+        wo_copy(t).wait()
+        terms[t] = lax.dot_general(ab[...], wo[t], NT, preferred_element_type=jnp.float32)
+        term_copy(t).start()
+
+    for t in range(n_o):
+        term_copy(t).wait_recv()
+        out_ref[:, t * O_CHUNK : (t + 1) * O_CHUNK] = (
+            terms[t, pl.ds(ours, 8), :] + other_terms[t]
+        ).astype(jnp.bfloat16)
+
+    for copy in sends:
+        copy.wait_send()
+    away.wait_send()
+    for t in range(n_o):
+        term_copy(t).wait_send()
+    for o in range(4):
+        itself = jnp.logical_and(c == half, mine == o)
+
+        @pl.when(jnp.logical_not(itself))
+        def _():
+            message(o).wait_send()
+
+
+def fused(tokens, query_weight, key_weight, value_weight, output_weight, key_cache, value_cache, lengths):
+    depth = tokens.shape[1]
+    n_q = query_weight.shape[0] // Q_CHUNK
+    n_o = output_weight.shape[0] // O_CHUNK
+    head_w = output_weight.shape[1]
+    anywhere = pl.BlockSpec(memory_space=pl.ANY)
+    in_vmem = pl.BlockSpec(memory_space=pltpu.VMEM)
+    f32, bf16, dma = jnp.float32, jnp.bfloat16, pltpu.SemaphoreType.DMA
+    return pl.pallas_call(
+        kernel,
+        out_shape=jax.ShapeDtypeStruct((GX, output_weight.shape[0]), bf16),
+        in_specs=[pl.BlockSpec(memory_space=pltpu.SMEM), in_vmem] + [anywhere] * 6,
+        out_specs=in_vmem,
+        scratch_shapes=[
+            pltpu.VMEM((n_q, Q_CHUNK, depth), bf16),
+            pltpu.VMEM((256, depth), bf16),
+            pltpu.VMEM((n_o, O_CHUNK, head_w), bf16),
+            pltpu.VMEM(key_cache.shape, bf16),
+            pltpu.VMEM(value_cache.shape, bf16),
+            pltpu.VMEM((TOK_ROWS, HD), f32),
+            pltpu.VMEM((GX * TOK_ROWS, HD), bf16),
+            pltpu.VMEM((GX * TOK_ROWS, HD), f32),
+            pltpu.VMEM((16, depth), bf16),
+            pltpu.VMEM((256, 128), f32),
+            pltpu.VMEM((128, 128), f32),
+            pltpu.VMEM((128, 128), bf16),
+            pltpu.VMEM((128, 128), bf16),
+            pltpu.VMEM((96, 128), f32),
+            pltpu.VMEM((GX * 96, 128), bf16),
+            pltpu.VMEM((GX * 96, 128), f32),
+            pltpu.VMEM((16, head_w), bf16),
+            pltpu.VMEM((n_o, 16, O_CHUNK), f32),
+            pltpu.VMEM((n_o, 8, O_CHUNK), f32),
+            dma((n_q,)), dma((2,)), dma((n_o,)), dma((2,)),
+            dma((7,)), dma((GX,)), dma((1,)), dma((1,)), dma((4,)), dma((4,)),
+            dma((7,)), dma((GX,)), dma((n_o,)), dma((n_o,)),
+        ],
+        compiler_params=pltpu.CompilerParams(
+            collective_id=0, has_side_effects=True, vmem_limit_bytes=60 * 2**20
+        ),
+        cost_estimate=pl.CostEstimate(
+            flops=1 << 30, bytes_accessed=54 << 20, transcendentals=1 << 15
+        ),
+    )(lengths, tokens, query_weight, key_weight, value_weight, output_weight, key_cache, value_cache)
+
+
+def fits_fused(tokens, query_weight, key_weight, output_weight, key_cache):
+    return (
+        lax.axis_size("gx") == GX
+        and lax.axis_size("gy") == 2
+        and tokens.shape == (2, TOK_ROWS * HD // 2)
+        and query_weight.shape[0] == 12 * HD
+        and key_weight.shape[0] == 96
+        and key_cache.shape == (2, 3, 256, HD)
+        and output_weight.shape == (2048, 48 * HD)
+    )
 
 
 def rotate(values, positions):
@@ -34,6 +347,10 @@
 def local(
     tokens, query_weight, key_weight, value_weight, output_weight, key_cache, value_cache, lengths
 ):
+    if fits_fused(tokens, query_weight, key_weight, output_weight, key_cache):
+        return fused(
+            tokens, query_weight, key_weight, value_weight, output_weight, key_cache, value_cache, lengths
+        )
     rows_here = tokens.shape[0]
     width_gx = lax.axis_size("gx")
     width_query = query_weight.shape[0]

time: 132 us -> 48.2 us (0.37)
  blocking collectives: 69.3 us -> 0 us
  Pallas kernels: 0 us -> 46.6 us
  matrix products: 27.5 us -> 0 us
  between operations: 13.5 us -> 0.01 us
  waiting for transfers between devices: 11.9 us -> 0 us
  starting transfers between devices: 5.5 us -> 0 us
  other arithmetic: 2.12 us -> 0 us
    all_gather x2 -> x0, blocking collectives: 65.5 us -> none  [the longest x1 34.9 us: local(): row_piece = lax.all_gather(tokens, 'gx', axis=0, tiled=True)]
    pallas_call x0 -> x1, Pallas kernels: none -> 46.6 us  [fused(): pl.pallas_call(kernel, out_shape=jax.ShapeDtypeStruct((GX, output_weight....]
    dot_general x7 -> x0, matrix products: 27.5 us -> none  [the longest x4 24.7 us: product(): lax.dot_general(row_piece, matrix, (((1,), (1,)), ((), ())), preferred_el...]
    all_to_all x1 -> x0, waiting for transfers between devices: 6.59 us -> none  [local(): lax.all_to_all(summed, 'gx', split_axis=0, concat_axis=1, tiled=True)]
    all_to_all x1 -> x0, starting transfers between devices: 5.46 us -> none  [local(): lax.all_to_all(summed, 'gx', split_axis=0, concat_axis=1, tiled=True)]
    reduce_scatter x1 -> x0, waiting for transfers between devices: 5.28 us -> none  [local(): lax.psum_scatter(terms, 'gy', scatter_dimension=0, tiled=True)]
    psum x1 -> x0, blocking collectives: 3.78 us -> none  [local(): summed = lax.psum(partial_value, 'gy').astype(jnp.bfloat16)]
    convert_element_type x5 -> x0, other arithmetic: 1.49 us -> none  [the longest x1 1.46 us: local(): lax.psum_scatter(terms, 'gy', scatter_dimension=0, tiled=True)]
  transfers between devices with their start and end apart: 2 -> 0, of which waited for: 2 -> 0; matrix products, arithmetic and copies ran while one was open for 0% -> 0% of each run, Pallas kernels for 0% -> 0%
where the time goes in v1:
time: 48.2 us; the launch traced here: 48 us
  Pallas kernels  46.6 us (97%)
  local copies, waits for them, and re-layouts  1.38 us (3%)
    pallas_call x1, Pallas kernels, fused(): pl.pallas_call(kernel, out_shape=jax.ShapeDtypeStruct((GX, output_weight....  46.6 us
    unnamed x1, local copies, waits for them, and re-layouts  1.38 us

profile of v1, /device:TPU:0, one launch (start us, length us, event | category | flops | bytes accessed | tf_op | source)
XLA Modules:
  0.0 48.0 jit_solution(446438187139289861)
XLA Ops:
  0.0 46.6 %shard_map.82 = bf16[8,2048]{1,0:T(8,128)(2,1)} custom-call(s32[2]{0:T(128)} %len_ref.1, bf16[2,8192]{1,0:T(2,128)(2,1)} %tok_ref.1, bf16[1536,8192]{1,0:T(8,128)(2,1)} %wq_hbm.1, bf16[96,8192]{1,0:T(8,128)(2,1)} %wk_hbm.1, bf16[96,8192]{1,0:T(8,128)(2,1)} %wv_hbm.1, bf16[2048,6144]{1,0:T(8,128)(2,1)} %wo_hbm.1, bf16[2,3,256,128]{3,2,1,0:T(8,128)(2,1)} %kc_hbm.1, ...), custom_call_target="tpu_custom_call" | custom-call | flops 1073741824 | bytes 56623104 | tf_op jit(solution)/shard_map/pallas_call | solution.py:276
  46.6 1.4 %copy.10 = bf16[8,2048]{1,0:T(8,128)(2,1)} copy(bf16[8,2048]{1,0:T(8,128)(2,1)} %shard_map.82) | data formatting | bytes 65536

commit v2 on v1

--- a/solution.py
+++ b/solution.py
@@ -15,55 +15,46 @@
 
 GX = 8
 TOK_ROWS = 128
-Q_CHUNK = 256
-O_CHUNK = 256
-
-
-def gather_start(buf, size, z, x, send, recv):
-    me = 2 * z + x
-    slot = buf.at[pl.ds(pl.multiple_of(me * size, size), size)]
-    copies = []
-    for d in (2, 1, 3):
-        copies.append(
-            pltpu.make_async_remote_copy(
-                slot, slot, send.at[d - 1], recv.at[me],
-                device_id={"gx": 2 * lax.rem(z + d, 4) + x}, device_id_type=MESH,
-            )
+Q_CHUNK = 512
+O_CHUNK = 512
+
+
+class Gather:
+    def __init__(self, buf, base, size, z, x, send, recv, n):
+        self.buf, self.base, self.size, self.z, self.x = buf, base, size, z, x
+        self.send, self.recv, self.n = send, recv, n
+
+    def slot_at(self, d, x):
+        return 2 * lax.rem(self.z + d, 4) + x
+
+    def copy(self, slot, sem, to):
+        rows = pl.ds(pl.multiple_of(self.base + slot * self.size, self.size), self.size)
+        block = self.buf.at[rows]
+        return pltpu.make_async_remote_copy(
+            block, block, self.send.at[7 * self.n + sem], self.recv.at[GX * self.n + slot],
+            device_id={"gx": to}, device_id_type=MESH,
         )
-    copies.append(
-        pltpu.make_async_remote_copy(
-            slot, slot, send.at[3], recv.at[me],
-            device_id={"gx": 2 * z + 1 - x}, device_id_type=MESH,
-        )
-    )
-    for copy in copies:
-        copy.start()
-    return copies
-
-
-def gather_finish(buf, size, z, x, send, recv):
-    other = 2 * z + 1 - x
-
-    def piece(s):
-        return buf.at[pl.ds(pl.multiple_of(s * size, size), size)]
-
-    copies = []
-    for d in (1, 3, 2):
-        s = 2 * lax.rem(z + d, 4) + x
-        copy = pltpu.make_async_remote_copy(
-            piece(s), piece(s), send.at[3 + d], recv.at[s],
-            device_id={"gx": other}, device_id_type=MESH,
-        )
-        copy.wait_recv()
-        copy.start()
-        copies.append(copy)
-    for d in range(4):
-        s = 2 * lax.rem(z + d, 4) + 1 - x
-        pltpu.make_async_remote_copy(
-            piece(s), piece(s), send.at[3], recv.at[s],
-            device_id={"gx": other}, device_id_type=MESH,
-        ).wait_recv()
-    return copies
+
+    def start(self):
+        me, over = self.slot_at(0, self.x), self.slot_at(0, 1 - self.x)
+        copies = [self.copy(me, d - 1, self.slot_at(d, self.x)) for d in (2, 1, 3)]
+        copies.append(self.copy(me, 3, over))
+        for copy in copies:
+            copy.start()
+        return copies
+
+    def forward(self):
+        over = self.slot_at(0, 1 - self.x)
+        copies = [self.copy(self.slot_at(d, self.x), 3 + d, over) for d in (1, 3, 2)]
+        for copy in copies:
+            copy.wait_recv()
+            copy.start()
+        return copies
+
+    def wait(self):
+        over = self.slot_at(0, 1 - self.x)
+        for d in range(4):
+            self.copy(self.slot_at(d, 1 - self.x), 3, over).wait_recv()
 
 
 def kernel(
@@ -98,19 +89,37 @@
     vc_copy.start()
 
     barrier = pltpu.get_barrier_semaphore()
-    for o in range(1, 2 * GX):
-        at = lax.rem(i * 2 + c + o, 2 * GX)
-        pl.semaphore_signal(
-            barrier, inc=1, device_id={"gx": at // 2, "gy": lax.rem(at, 2)}, device_id_type=MESH
-        )
+    def greet(gx, gy):
+        pl.semaphore_signal(barrier, inc=1, device_id={"gx": gx, "gy": gy}, device_id_type=MESH)
+
+    mine = lax.rem(i, 4)
+    greet(i, 1 - c)
+    greet(2 * z + 1 - x, c)
+    for d in range(1, 4):
+        greet(2 * lax.rem(z + d, 4) + x, c)
+    for o in range(4):
+
+        @pl.when(jnp.logical_not(jnp.logical_and(c == half, mine == o)))
+        def _():
+            greet(4 * c + o, half)
+
     tok = tok_ref[...].astype(jnp.float32)
     pieces = tok.shape[1] // HD
     for k in range(pieces):
         tok_f[pl.ds(k, 2, stride=pieces), :] = tok[:, k * HD : (k + 1) * HD]
     xr[pl.ds(pl.multiple_of(i * TOK_ROWS, TOK_ROWS), TOK_ROWS), :] = tok_f[...].astype(jnp.bfloat16)
-    pl.semaphore_wait(barrier, 2 * GX - 1)
-
-    sends = gather_start(xr, TOK_ROWS, z, x, x_send, x_recv)
+
+    @pl.when(c == half)
+    def _():
+        pl.semaphore_wait(barrier, 8)
+
+    @pl.when(c != half)
+    def _():
+        pl.semaphore_wait(barrier, 9)
+
+
+    tok_gather = Gather(xr, 0, TOK_ROWS, z, x, x_send, x_recv, 0)
+    sends = tok_gather.start()
     wkv[kw:128, :] = jnp.zeros((128 - kw, wkv.shape[1]), jnp.bfloat16)
     wkv[128 + kw : 256, :] = jnp.zeros((128 - kw, wkv.shape[1]), jnp.bfloat16)
     lane = lax.broadcasted_iota(jnp.int32, (8, HD), 1)
@@ -122,7 +131,8 @@
     cosine = jnp.cos(angles)
     sine = jnp.sin(angles)
     sine = jnp.where(lane < HD // 2, -sine, sine)
-    sends += gather_finish(xr, TOK_ROWS, z, x, x_send, x_recv)
+    sends += tok_gather.forward()
+    tok_gather.wait()
 
     xf[...] = xr[...].astype(jnp.float32)
     for k in range(pieces):
@@ -160,8 +170,6 @@
     away.wait_recv()
     summed[...] = (part[pl.ds(pl.multiple_of(c * 128, 128), 128), :] + other_part[...]).astype(jnp.bfloat16)
 
-    mine = lax.rem(i, 4)
-
     def message(o):
         return pltpu.make_async_remote_copy(
             summed.at[pl.ds(o * 32, 32)], got.at[pl.ds(pl.multiple_of(mine * 32, 32), 32)],
@@ -190,6 +198,7 @@
     for s in range(4):
         message_here(s).wait()
     scale = HD ** (-0.5)
+    rows = []
     for r in range(2):
         keys, values = [], []
         for s in range(4):
@@ -197,11 +206,13 @@
             qs[r * 48 + 12 * s : r * 48 + 12 * s + 12, :] = block[0:12, :]
             keys.append(block[12:13, :kw])
             values.append(block[13:14, :kw])
-        keys = jnp.concatenate(keys, axis=1)
-        values = jnp.concatenate(values, axis=1)
-        cos_r = cosine[r : r + 1, :]
-        sin_r = sine[r : r + 1, :]
-        for g in range(3):
+        rows.append((jnp.concatenate(keys, axis=1), jnp.concatenate(values, axis=1)))
+    gathers = []
+    for g in range(3):
+        for r in range(2):
+            keys, values = rows[r]
+            cos_r = cosine[r : r + 1, :]
+            sin_r = sine[r : r + 1, :]
             k_new = keys[:, g * HD : (g + 1) * HD]
             v_new = values[:, g * HD : (g + 1) * HD]
             k_rot = (k_new * cos_r + pltpu.roll(k_new, HD // 2, 1) * sin_r).astype(jnp.bfloat16)
@@ -223,13 +234,11 @@
             own_weight = (own_exp / total).astype(jnp.bfloat16).astype(jnp.float32)
             mixed = jnp.dot(weights, vc[r, g], preferred_element_type=jnp.float32)
             mixed = mixed + own_weight * v_new
-            ag[pl.ds(pl.multiple_of(i * 96 + r * 48 + 16 * g, 16), 16), :] = mixed.astype(jnp.bfloat16)
-
-    sends += gather_start(ag, 96, z, x, a_send, a_recv)
-    sends += gather_finish(ag, 96, z, x, a_send, a_recv)
-    agf[...] = ag[...].astype(jnp.float32)
-    for h in range(48):
-        ab[:, h * HD : (h + 1) * HD] = agf[pl.ds(h, 16, stride=48), :].astype(jnp.bfloat16)
+            ag[pl.ds(pl.multiple_of(g * 256 + i * 32 + r * 16, 16), 16), :] = mixed.astype(jnp.bfloat16)
+        gathers.append(Gather(ag, g * 256, 32, z, x, a_send, a_recv, g))
+        sends += gathers[g].start()
+    for gather in gathers:
+        sends += gather.forward()
 
     theirs = pl.multiple_of((1 - c) * 8, 8)
     ours = pl.multiple_of(c * 8, 8)
@@ -240,11 +249,23 @@
             device_id={"gy": 1 - c}, device_id_type=MESH,
         )
 
-    @pl.loop(0, n_o)
-    def _(t):
-        wo_copy(t).wait()
-        terms[t] = lax.dot_general(ab[...], wo[t], NT, preferred_element_type=jnp.float32)
-        term_copy(t).start()
+    width = 16 * HD
+    for g in range(3):
+        gathers[g].wait()
+        agf[...] = ag[g * 256 : (g + 1) * 256, :].astype(jnp.float32)
+        for h in range(16):
+            ab[:, h * HD : (h + 1) * HD] = agf[pl.ds(h, 16, stride=16), :].astype(jnp.bfloat16)
+
+        @pl.loop(0, n_o)
+        def _(t):
+            if g == 0:
+                wo_copy(t).wait()
+            value = lax.dot_general(
+                ab[...], wo[t, :, g * width : (g + 1) * width], NT, preferred_element_type=jnp.float32
+            )
+            terms[t] = value if g == 0 else terms[t] + value
+            if g == 2:
+                term_copy(t).start()
 
     for t in range(n_o):
         term_copy(t).wait_recv()
@@ -294,13 +315,13 @@
             pltpu.VMEM((128, 128), bf16),
             pltpu.VMEM((96, 128), f32),
             pltpu.VMEM((GX * 96, 128), bf16),
-            pltpu.VMEM((GX * 96, 128), f32),
-            pltpu.VMEM((16, head_w), bf16),
+            pltpu.VMEM((GX * 32, 128), f32),
+            pltpu.VMEM((16, 16 * HD), bf16),
             pltpu.VMEM((n_o, 16, O_CHUNK), f32),
             pltpu.VMEM((n_o, 8, O_CHUNK), f32),
             dma((n_q,)), dma((2,)), dma((n_o,)), dma((2,)),
             dma((7,)), dma((GX,)), dma((1,)), dma((1,)), dma((4,)), dma((4,)),
-            dma((7,)), dma((GX,)), dma((n_o,)), dma((n_o,)),
+            dma((21,)), dma((3 * GX,)), dma((n_o,)), dma((n_o,)),
         ],
         compiler_params=pltpu.CompilerParams(
             collective_id=0, has_side_effects=True, vmem_limit_bytes=60 * 2**20

time: 48.2 us -> 46 us (0.954)
  Pallas kernels: 46.6 us -> 44.4 us
    pallas_call x1, Pallas kernels: 46.6 us -> 44.4 us  [fused(): pl.pallas_call(kernel, out_shape=jax.ShapeDtypeStruct((GX, output_weight....]
where the time goes in v2:
time: 46 us; the launch traced here: 45.7 us
  Pallas kernels  44.4 us (97%)
  local copies, waits for them, and re-layouts  1.38 us (3%)
    pallas_call x1, Pallas kernels, fused(): pl.pallas_call(kernel, out_shape=jax.ShapeDtypeStruct((GX, output_weight....  44.4 us
    unnamed x1, local copies, waits for them, and re-layouts  1.38 us

profile of v2, /device:TPU:0, one launch (start us, length us, event | category | flops | bytes accessed | tf_op | source)
XLA Modules:
  0.0 45.7 jit_solution(11313355037159236493)
XLA Ops:
  0.0 44.4 %shard_map.82 = bf16[8,2048]{1,0:T(8,128)(2,1)} custom-call(s32[2]{0:T(128)} %len_ref.1, bf16[2,8192]{1,0:T(2,128)(2,1)} %tok_ref.1, bf16[1536,8192]{1,0:T(8,128)(2,1)} %wq_hbm.1, bf16[96,8192]{1,0:T(8,128)(2,1)} %wk_hbm.1, bf16[96,8192]{1,0:T(8,128)(2,1)} %wv_hbm.1, bf16[2048,6144]{1,0:T(8,128)(2,1)} %wo_hbm.1, bf16[2,3,256,128]{3,2,1,0:T(8,128)(2,1)} %kc_hbm.1, ...), custom_call_target="tpu_custom_call" | custom-call | flops 1073741824 | bytes 56623104 | tf_op jit(solution)/shard_map/pallas_call | solution.py:297
  44.4 1.4 %copy.10 = bf16[8,2048]{1,0:T(8,128)(2,1)} copy(bf16[8,2048]{1,0:T(8,128)(2,1)} %shard_map.82) | data formatting | bytes 65536

commit v3 on v2

--- a/solution.py
+++ b/solution.py
@@ -235,6 +235,7 @@
             mixed = jnp.dot(weights, vc[r, g], preferred_element_type=jnp.float32)
             mixed = mixed + own_weight * v_new
             ag[pl.ds(pl.multiple_of(g * 256 + i * 32 + r * 16, 16), 16), :] = mixed.astype(jnp.bfloat16)
+    for g in range(3):
         gathers.append(Gather(ag, g * 256, 32, z, x, a_send, a_recv, g))
         sends += gathers[g].start()
     for gather in gathers:

time: 46 us -> 47.3 us (1.028)
  Pallas kernels: 44.4 us -> 45.7 us
    pallas_call x1, Pallas kernels: 44.4 us -> 45.7 us  [fused(): pl.pallas_call(kernel, out_shape=jax.ShapeDtypeStruct((GX, output_weight....]
where the time goes in v3:
time: 47.3 us; the launch traced here: 47 us
  Pallas kernels  45.7 us (97%)
  local copies, waits for them, and re-layouts  1.38 us (3%)
    pallas_call x1, Pallas kernels, fused(): pl.pallas_call(kernel, out_shape=jax.ShapeDtypeStruct((GX, output_weight....  45.7 us
    unnamed x1, local copies, waits for them, and re-layouts  1.38 us

profile of v3, /device:TPU:0, one launch (start us, length us, event | category | flops | bytes accessed | tf_op | source)
XLA Modules:
  0.0 47.0 jit_solution(5094546728810080058)
XLA Ops:
  0.0 45.7 %shard_map.82 = bf16[8,2048]{1,0:T(8,128)(2,1)} custom-call(s32[2]{0:T(128)} %len_ref.1, bf16[2,8192]{1,0:T(2,128)(2,1)} %tok_ref.1, bf16[1536,8192]{1,0:T(8,128)(2,1)} %wq_hbm.1, bf16[96,8192]{1,0:T(8,128)(2,1)} %wk_hbm.1, bf16[96,8192]{1,0:T(8,128)(2,1)} %wv_hbm.1, bf16[2048,6144]{1,0:T(8,128)(2,1)} %wo_hbm.1, bf16[2,3,256,128]{3,2,1,0:T(8,128)(2,1)} %kc_hbm.1, ...), custom_call_target="tpu_custom_call" | custom-call | flops 1073741824 | bytes 56623104 | tf_op jit(solution)/shard_map/pallas_call | solution.py:298
  45.7 1.4 %copy.10 = bf16[8,2048]{1,0:T(8,128)(2,1)} copy(bf16[8,2048]{1,0:T(8,128)(2,1)} %shard_map.82) | data formatting | bytes 65536
